TPU v7x, 512 devices: a whole 4x4x16 slice. The times are simulated.
512 devices in a mesh: req: 32 (over y, z_lo), head: 16 (over x, z_hi, core).
Axes of the slice: x: 4, y: 4, z: 16 (z_hi: 2, z_lo: 8; z = z_hi * 8 + z_lo), core: 2. Of those that a mesh axis runs over, the one named last changes fastest.
Arguments:
- hidden: bfloat16 [256, 2048], P('req', 'head'), may hold values from -6 to 6
- attn_gain: float32 [2048], replicated, may hold values from 0.1 to 1.9
- q_weight: bfloat16 [2048, 2048], P(None, 'head'), may hold values from -0.125 to 0.125
- gate_weight: bfloat16 [2048, 2048], P(None, 'head'), may hold values from -0.125 to 0.125
- key_value_weight: bfloat16 [2048, 2048], P(None, 'head'), may hold values from -0.125 to 0.125
- q_gain: float32 [128], replicated, may hold values from 0.5 to 1.5
- k_gain: float32 [128], replicated, may hold values from 0.5 to 2
- out_weight: bfloat16 [2048, 2048], P('head'), may hold values from -0.5 to 0.5
- prompt_key_cache: bfloat16 [32, 4096, 8, 128], P('req', 'head'), may hold values from -3.5 to 3.5
- prompt_value_cache: bfloat16 [32, 4096, 8, 128], P('req', 'head'), may hold values from -6 to 6
- tail_key_cache: bfloat16 [32, 4, 256, 8, 128], P('req', None, 'head'), may hold values from -3.5 to 3.5
- tail_value_cache: bfloat16 [32, 4, 256, 8, 128], P('req', None, 'head'), may hold values from -6 to 6
- mlp_gain: float32 [2048], replicated, may hold values from 0.1 to 1.9
- mlp_gate: bfloat16 [2048, 6144], P('req', 'head'), may hold values from -0.125 to 0.125
- mlp_up: bfloat16 [2048, 6144], P('req', 'head'), may hold values from -0.125 to 0.125
- mlp_down: bfloat16 [6144, 2048], P('head'), may hold values from -0.109375 to 0.109375
- final_gain: float32 [2048], P('head'), may hold values from 0.1 to 1.9
- score_weight: float32 [2048], P('head'), may hold values from -0.125 to 0.125
- prompt_lengths: int32 [32], replicated, may hold values from 1 to 4096, 65536 in all
- tail_lengths: int32 [32, 4], replicated, may hold values from 1 to 256, 512 in all within a row
- group_prompt: int32 [32], replicated, may hold values from 0 to 31, each once
Outputs:
- new_hidden: bfloat16 [256, 2048], P('req', 'head')
- score: float32 [256], P('req')
Inputs may be any that keep to these rules, and one draw needn't show every extreme that they name: `group_prompt`: every prompt is held by exactly one group. `prompt_lengths`: one prompt has exactly 4096 prefix tokens. `tail_lengths`: in every prompt one continuation has exactly 256 tail tokens.
All inputs are finite; a program needn't handle non-finite values.
Results may differ from a plain program's by a relative error of at most 0.023.
Values may be sent and summed in bfloat16 or wider, within the bound.
A program may use at most 64 MiB of HBM per device.

v0:
```python
import math
import jax
import jax.numpy as jnp
from jax import lax
from jax.sharding import PartitionSpec as P

EPS = 1e-06
THETA = 1000000.0


def rms_scale(value, gain):
    return value * lax.rsqrt(jnp.mean(value * value, axis=-1, keepdims=True) + EPS) * gain


def rotate(value, position):
    head_width = value.shape[-1]
    half_width = head_width // 2
    frequency = jnp.exp(
        -math.log(THETA) * 2.0 * jnp.arange(half_width, dtype=jnp.float32) / head_width
    )
    angles = position.astype(jnp.float32)[:, None] * frequency[None, :]
    cosine = jnp.cos(angles)[:, None, :]
    sine_part = jnp.sin(angles)[:, None, :]
    first_half = value[..., :half_width]
    second_half = value[..., half_width:]
    return jnp.concatenate(
        [
            first_half * cosine - second_half * sine_part,
            second_half * cosine + first_half * sine_part,
        ],
        axis=-1,
    )


def shards(
    hidden,
    attn_gain,
    q_weight,
    gate_weight,
    key_value_weight,
    q_gain,
    k_gain,
    out_weight,
    prompt_key_cache,
    prompt_value_cache,
    tail_key_cache,
    tail_value_cache,
    mlp_gain,
    mlp_gate,
    mlp_up,
    mlp_down,
    final_gain,
    score_weight,
    prompt_lengths,
    tail_lengths,
    group_prompt,
):
    head_count = lax.axis_size("head")
    group_count = lax.axis_size("req")
    group_id = lax.axis_index("req")
    head_place = lax.axis_index("head")
    count_of_rows = hidden.shape[0]
    model_width = attn_gain.shape[0]
    head_width = q_gain.shape[0]
    own_heads = q_weight.shape[1] // head_width
    all_heads = own_heads * head_count
    block_count = key_value_weight.shape[1] // head_width
    kv_heads = block_count * head_count // 2
    sharing_count = all_heads // kv_heads
    cont_count = tail_lengths.shape[1]
    new_count = count_of_rows // cont_count
    score_scale = 1.0 / math.sqrt(head_width)
    slot_ids = jnp.arange(group_count, dtype=jnp.int32)
    prompt_id = jnp.sum(jnp.where(slot_ids == group_id, group_prompt, 0))
    prompt_len = jnp.sum(jnp.where(slot_ids == prompt_id, prompt_lengths, 0))
    tail_row = jnp.sum(jnp.where((slot_ids == prompt_id)[:, None], tail_lengths, 0), axis=0)
    owner_group = jnp.sum(
        jnp.where(group_prompt[None, :] == slot_ids[:, None], slot_ids[None, :], 0), axis=1
    )
    position = (
        prompt_len + tail_row[:, None] + jnp.arange(new_count, dtype=jnp.int32)[None, :]
    ).reshape(count_of_rows)
    whole_rows = lax.all_gather(hidden, "head", axis=1, tiled=True)
    block_rows = whole_rows.astype(jnp.float32)
    normalized_hidden = rms_scale(block_rows, attn_gain).astype(jnp.bfloat16)
    gate_pre = jnp.dot(normalized_hidden, gate_weight, preferred_element_type=jnp.float32)
    query_rows = jnp.dot(normalized_hidden, q_weight, preferred_element_type=jnp.float32).reshape(
        count_of_rows, own_heads, head_width
    )
    query_rows = rotate(rms_scale(query_rows, q_gain), position).astype(jnp.bfloat16)
    projected_rows = jnp.dot(
        normalized_hidden, key_value_weight, preferred_element_type=jnp.float32
    ).reshape(count_of_rows, block_count, head_width)
    is_key = (head_place * block_count + jnp.arange(block_count, dtype=jnp.int32)) % 2 == 0
    keyed = rotate(rms_scale(projected_rows, k_gain), position)
    fresh = jnp.where(is_key[None, :, None], keyed, projected_rows).astype(jnp.bfloat16)
    all_queries, all_fresh = (
        lax.all_gather(
            query_rows.reshape(count_of_rows, own_heads * head_width), "head", axis=1, tiled=True
        ),
        lax.all_gather(
            fresh.reshape(count_of_rows, block_count * head_width), "head", axis=1, tiled=True
        ),
    )
    query_groups = all_queries.reshape(count_of_rows, kv_heads, sharing_count, head_width)
    local_keys = prompt_key_cache[0]
    local_values = prompt_value_cache[0]
    span_length = local_keys.shape[0]
    block_size = min(128, span_length)
    block_total = span_length // block_size
    span_start = head_place * span_length

    def prefix_block(block_id, sums):
        numer_acc, total_acc = sums
        key_block = lax.dynamic_slice_in_dim(local_keys, block_id * block_size, block_size, 0)
        value_block = lax.dynamic_slice_in_dim(local_values, block_id * block_size, block_size, 0)
        scores = (
            jnp.einsum(
                "rkgd,tkd->rkgt", query_groups, key_block, preferred_element_type=jnp.float32
            )
            * score_scale
        )
        slot_pos = span_start + block_id * block_size + jnp.arange(block_size, dtype=jnp.int32)
        attention_weights = jnp.where(
            slot_pos[None, None, None, :] < prompt_len, jnp.exp(scores), 0.0
        )
        numer_acc = numer_acc + jnp.einsum(
            "rkgt,tkd->rkgd",
            attention_weights.astype(jnp.bfloat16),
            value_block,
            preferred_element_type=jnp.float32,
        )
        return (numer_acc, total_acc + jnp.sum(attention_weights, axis=-1))

    start_sums = (
        jnp.zeros((count_of_rows, kv_heads, sharing_count, head_width), jnp.float32),
        jnp.zeros((count_of_rows, kv_heads, sharing_count), jnp.float32),
    )
    numerator, denominator = lax.fori_loop(0, block_total, prefix_block, start_sums)
    continuation_rows = query_groups.reshape(
        cont_count, new_count, kv_heads, sharing_count, head_width
    )
    tkeys = tail_key_cache[0]
    tail_value_rows = tail_value_cache[0]
    tail_span = tkeys.shape[1]
    scores = (
        jnp.einsum(
            "cjkgd,ctkd->cjkgt", continuation_rows, tkeys, preferred_element_type=jnp.float32
        )
        * score_scale
    )
    tail_pos = head_place * tail_span + jnp.arange(tail_span, dtype=jnp.int32)
    tail_live = tail_pos[None, :] < tail_row[:, None]
    attention_weights = jnp.where(tail_live[:, None, None, None, :], jnp.exp(scores), 0.0)
    numerator = numerator + jnp.einsum(
        "ihbyw,iwbs->ihbys",
        attention_weights.astype(jnp.bfloat16),
        tail_value_rows,
        preferred_element_type=jnp.float32,
    ).reshape(count_of_rows, kv_heads, sharing_count, head_width)
    denominator = denominator + jnp.sum(attention_weights, axis=-1).reshape(
        count_of_rows, kv_heads, sharing_count
    )
    numerator = numerator.reshape(count_of_rows, all_heads, head_width)
    denominator = denominator.reshape(count_of_rows, all_heads)
    numer_sum, total_sum = lax.psum((numerator, denominator), "head")
    numer_own = lax.dynamic_slice_in_dim(numer_sum, head_place * own_heads, own_heads, 1)
    total_own = lax.dynamic_slice_in_dim(total_sum, head_place * own_heads, own_heads, 1)
    fresh_all = all_fresh.reshape(count_of_rows, kv_heads, 2, head_width)
    own_kv = max(own_heads // sharing_count, 1)
    per_kv = own_heads // own_kv
    nearby = lax.dynamic_slice_in_dim(fresh_all, head_place * own_heads // sharing_count, own_kv, 1)
    own_queries = query_rows.reshape(cont_count, new_count, own_kv, per_kv, head_width)
    recent_key_rows = nearby[:, :, 0].reshape(cont_count, new_count, own_kv, head_width)
    recent_value_rows = nearby[:, :, 1].reshape(cont_count, new_count, own_kv, head_width)
    scores = (
        jnp.einsum(
            "cjkgd,cukd->cjkgu", own_queries, recent_key_rows, preferred_element_type=jnp.float32
        )
        * score_scale
    )
    causal = (
        jnp.arange(new_count, dtype=jnp.int32)[None, :]
        <= jnp.arange(new_count, dtype=jnp.int32)[:, None]
    )
    attention_weights = jnp.where(causal[None, :, None, None, :], jnp.exp(scores), 0.0)
    numer_own = numer_own + jnp.einsum(
        "bfmne,beml->bfmnl",
        attention_weights.astype(jnp.bfloat16),
        recent_value_rows,
        preferred_element_type=jnp.float32,
    ).reshape(count_of_rows, own_heads, head_width)
    total_own = total_own + jnp.sum(attention_weights, axis=-1).reshape(count_of_rows, own_heads)
    attention = (numer_own / total_own[..., None]).reshape(count_of_rows, own_heads * head_width)
    gated = (attention * jax.nn.sigmoid(gate_pre)).astype(jnp.bfloat16)
    mixed = lax.psum(jnp.dot(gated, out_weight, preferred_element_type=jnp.float32), "head")
    attended = (block_rows + mixed).astype(jnp.bfloat16)
    col_width = model_width // head_count
    wide_rows = attended.astype(jnp.float32)
    mlp_in = rms_scale(wide_rows, mlp_gain).astype(jnp.bfloat16)
    column_in = lax.all_to_all(mlp_in, "req", split_axis=1, concat_axis=0, tiled=True)
    gate_part = jnp.dot(column_in, mlp_gate, preferred_element_type=jnp.float32)
    up_part = jnp.dot(column_in, mlp_up, preferred_element_type=jnp.float32)
    gate_own, up_own = (
        lax.psum_scatter(gate_part, "req", scatter_dimension=0, tiled=True),
        lax.psum_scatter(up_part, "req", scatter_dimension=0, tiled=True),
    )
    act_rows = (jax.nn.silu(gate_own) * up_own).astype(jnp.bfloat16)
    down_part = jnp.dot(act_rows, mlp_down, preferred_element_type=jnp.float32)
    down_total = lax.psum(down_part, "head")
    added = lax.dynamic_slice_in_dim(down_total, head_place * col_width, col_width, 1)
    residual = lax.dynamic_slice_in_dim(wide_rows, head_place * col_width, col_width, 1)
    finished = (residual + added).astype(jnp.bfloat16)
    everyone = lax.all_gather(finished, "req", axis=0, tiled=True)
    my_owner = jnp.sum(jnp.where(slot_ids == group_id, owner_group, 0))
    new_hidden = lax.dynamic_slice_in_dim(everyone, my_owner * count_of_rows, count_of_rows, 0)
    final_rows = new_hidden.astype(jnp.float32)
    squares, product = lax.psum(
        (
            jnp.sum(final_rows * final_rows, axis=-1),
            jnp.sum(final_rows * final_gain * score_weight, axis=-1),
        ),
        "head",
    )
    score = product * lax.rsqrt(squares / model_width + EPS)
    return (new_hidden, score)


def solution(mesh):
    return jax.shard_map(
        shards,
        mesh=mesh,
        in_specs=(
            P("req", "head"),
            P(),
            P(None, "head"),
            P(None, "head"),
            P(None, "head"),
            P(),
            P(),
            P("head", None),
            P("req", "head", None, None),
            P("req", "head", None, None),
            P("req", None, "head", None, None),
            P("req", None, "head", None, None),
            P(),
            P("req", "head"),
            P("req", "head"),
            P("head", None),
            P("head"),
            P("head"),
            P(),
            P(),
            P(),
        ),
        out_specs=(P("req", "head"), P("req")),
        check_vma=False,
    )
```

profile of v0, /device:TPU:1, one launch (start us, length us, event | category | flops | bytes accessed | tf_op | source)
XLA Modules:
  0.0 1502.3 jit_solution(17086110039047880849)
XLA Ops:
  7.3 51.2 %all_gather.12 = bf16[8,2048]{1,0:T(8,128)(2,1)S(1)} all-gather(bf16[8,128]{1,0:T(8,128)(2,1)} %param.23), channel_id=1, replica_groups=mesh['req'=32,'head'=16] {'head'}, dimensions={1}, use_global_device_ids=true | all-gather | bytes 34816 | tf_op jit(solution)/shard_map/all_gather | solution.py:83
  58.6 0.8 select_reduce_fusion
  59.3 1.3 fusion.70
  60.6 0.6 iota_compare_fusion.2
  61.3 2.0 select_reduce_fusion.2
  63.3 0.8 select_reduce_fusion.1
  64.1 0.7 broadcast_add_fusion
  65.0 1.4 multiply_reduce_fusion.2
  66.4 0.7 multiply_bitcast_fusion.1
  67.3 33.8 %all_gather.13 = bf16[8,2048]{1,0:T(8,128)(2,1)S(1)} all-gather(bf16[8,128]{1,0:T(8,128)(2,1)S(1)} %pad_maximum_fusion), channel_id=1, replica_groups=mesh['req'=32,'head'=16] {'head'}, dimensions={1}, use_global_device_ids=true | all-gather | bytes 34816 | tf_op jit(solution)/shard_map/all_gather | solution.py:98
  101.1 1.4 copy_bitcast_fusion
  102.6 2.6 while.16
  102.6 0.8 add_compare_fusion.2
  103.9 0.7 add_compare_fusion.2
  105.6 1.1 convolution_bitcast_fusion.1
  108.2 43.8 %all_gather.14 = bf16[8,2048]{1,0:T(8,128)(2,1)S(1)} all-gather(bf16[8,128]{1,0:T(8,128)(2,1)S(1)} %fusion.57), channel_id=1, replica_groups=mesh['req'=32,'head'=16] {'head'}, dimensions={1}, use_global_device_ids=true | all-gather | bytes 34816 | tf_op jit(solution)/shard_map/all_gather | solution.py:101
  153.0 62.0 %psum.43 = f32[8,16]{0,1:T(8,128)S(1)} all-reduce(f32[8,16]{0,1:T(8,128)S(1)} %bitcast.127), channel_id=1, replica_groups=mesh['req'=32,'head'=16] {'head'}, use_global_device_ids=true, to_apply=%region_11.12 | all-reduce | flops 128 | bytes 1024 | tf_op jit(solution)/shard_map/psum | solution.py:166
  215.2 132.7 %all-reduce.9.cloned.1.call-done = f32[8,16,128]{2,0,1:T(8,128)} async-done(((f32[8,16,128]{2,0,1:T(8,128)}), f32[8,16,128]{2,0,1:T(8,128)}) %all-reduce.9.cloned.1.call-update) | async-done | bytes 65552 | tf_op jit(solution)/shard_map/psum | solution.py:166
  347.9 1.7 fusion.20
  349.7 242.6 %all-reduce.11.cloned.1.call-done = f32[8,2048]{1,0:T(8,128)} async-done(((f32[8,2048]{1,0:T(8,128)}), f32[8,2048]{1,0:T(8,128)}) %all-reduce.11.cloned.1.call-update) | async-done | bytes 65552 | tf_op jit(solution)/shard_map/psum | solution.py:196
  592.3 1.0 multiply_reduce_fusion
  593.7 16.2 %all_to_all.19 = bf16[32,2,256]{2,1,0:T(2,128)(2,1)S(1)} all-to-all(bf16[32,2,256]{2,1,0:T(2,128)(2,1)S(1)} %reshape.325), channel_id=1, replica_groups=mesh['req'=32,'head'=16] {'req'}, dimensions={0} | all-to-all | bytes 65536 | tf_op jit(solution)/shard_map/all_to_all | solution.py:201
  610.1 0.9 fusion.27
  611.0 1.0 fusion.29
  612.0 1.3 dynamic-slice
  613.9 428.9 %all-reduce.15.cloned.1.call-done = (f32[256,384]{1,0:T(8,128)}, f32[256,384]{1,0:T(8,128)}) async-done(((f32[256,384]{1,0:T(8,128)}, f32[256,384]{1,0:T(8,128)}), (f32[256,384]{1,0:T(8,128)}, f32[256,384]{1,0:T(8,128)})) %all-reduce.15.cloned.1.call-update) | async-done | bytes 786448
  1042.8 1.7 fusion.35
  1045.2 263.3 %all-reduce.13.cloned.1.call-done = f32[8,2048]{1,0:T(8,128)} async-done(((f32[8,2048]{1,0:T(8,128)}), f32[8,2048]{1,0:T(8,128)}) %all-reduce.13.cloned.1.call-update) | async-done | bytes 65552 | tf_op jit(solution)/shard_map/psum | solution.py:210
  1308.5 0.7 add_convert_fusion
  1309.2 101.1 %all_gather.15 = bf16[256,128]{1,0:T(8,128)(2,1)S(1)} all-gather(bf16[8,128]{1,0:T(8,128)(2,1)S(1)} %add_convert_fusion), channel_id=1, replica_groups=mesh['req'=32,'head'=16] {'req'}, dimensions={0}, use_global_device_ids=true | all-gather | bytes 67584 | tf_op jit(solution)/shard_map/all_gather | solution.py:214
  1410.2 0.7 fusion.48
  1411.0 84.3 %all-reduce.3 = (f32[8]{0:T(128)S(1)}, f32[8]{0:T(128)S(1)}) all-reduce(f32[8]{0:T(128)S(1)} %get-tuple-element.172, f32[8]{0:T(128)S(1)} %get-tuple-element.171), channel_id=1, replica_groups=mesh['req'=32,'head'=16] {'head'}, use_global_device_ids=true, to_apply=%region_21.22 | all-reduce | flops 16 | bytes 128 | tf_op jit(solution)/shard_map/psum | solution.py:218
  (82 shorter events, 5.7 us)
Async XLA Ops:
  7.2 1035.7 %copy-start = (bf16[384,2048]{1,0:T(8,128)(2,1)S(1)}, bf16[384,2048]{1,0:T(8,128)(2,1)}, u32[]{:S(2)}) copy-start(bf16[384,2048]{1,0:T(8,128)(2,1)} %param.38) | copy-start | bytes 4718596
  7.2 340.7 %all-reduce.9.cloned.1.call-start = ((), (), s32[]{:S(2)}) async-start(), calls=%async_computation.1 | async-start | bytes 131072 | tf_op jit(solution)/shard_map/psum | solution.py:166
  102.5 2.8 copy-start.11
  102.5 5.0 copy-start.3
  102.5 5.0 copy-start.4
  105.2 2.8 copy-start.8
  105.2 242.7 %copy-start.1 = (bf16[128,2048]{1,0:T(8,128)(2,1)S(1)}, bf16[128,2048]{1,0:T(8,128)(2,1)}, u32[]{:S(2)}) copy-start(bf16[128,2048]{1,0:T(8,128)(2,1)} %param.30) | copy-start | bytes 1572868
  105.2 242.7 %copy-start.2 = (bf16[2048,128]{1,0:T(8,128)(2,1)S(1)}, bf16[2048,128]{1,0:T(8,128)(2,1)}, u32[]{:S(2)}) copy-start(bf16[2048,128]{1,0:T(8,128)(2,1)} %param.26) | copy-start | bytes 1572868
  105.6 487.7 %copy-start.7 = (f32[2048]{0:T(1024)S(1)}, f32[2048]{0:T(1024)}, u32[]{:S(2)}) copy-start(f32[2048]{0:T(1024)} %param.35) | copy-start | bytes 24580
  106.8 503.3 %copy-start.5 = (bf16[64,384]{1,0:T(8,128)(2,1)S(1)}, bf16[64,384]{1,0:T(8,128)(2,1)}, u32[]{:S(2)}) copy-start(bf16[64,384]{1,0:T(8,128)(2,1)} %param.37) | copy-start | bytes 147460
  107.4 484.9 %all-reduce.11.cloned.1.call-start = ((), (), s32[]{:S(2)}) async-start(), calls=%async_computation.2 | async-start | bytes 131072 | tf_op jit(solution)/shard_map/psum | solution.py:196
  107.6 503.4 %copy-start.6 = (bf16[64,384]{1,0:T(8,128)(2,1)S(1)}, bf16[64,384]{1,0:T(8,128)(2,1)}, u32[]{:S(2)}) copy-start(bf16[64,384]{1,0:T(8,128)(2,1)} %param.36) | copy-start | bytes 147460
  349.7 693.2 %all-reduce.15.cloned.1.call-start = ((), (), s32[]{:S(2)}) async-start(), calls=%async_computation.4 | async-start | bytes 1572864
  611.0 799.3 %copy-start.9 = (f32[128]{0:T(128)S(1)}, f32[128]{0:T(128)}, u32[]{:S(2)}) copy-start(f32[128]{0:T(128)} %param.40) | copy-start | bytes 1540
  611.0 799.3 %copy-start.10 = (f32[128]{0:T(128)S(1)}, f32[128]{0:T(128)}, u32[]{:S(2)}) copy-start(f32[128]{0:T(128)} %param.39) | copy-start | bytes 1540
  612.0 696.5 %all-reduce.13.cloned.1.call-start = ((), (), s32[]{:S(2)}) async-start(), calls=%async_computation.3 | async-start | bytes 131072 | tf_op jit(solution)/shard_map/psum | solution.py:210
Sparse Core Ops, SparseCore 0:
  107.6 240.3 all-reduce.8
  351.1 241.2 all-reduce.10
  612.1 430.6 all-reduce.14
  1045.9 262.5 all-reduce.12
where the time goes:
time: 1500 us
  waiting for transfers between devices  1070 us (71%)
  blocking collectives  392 us (26%)
  between operations  15.4 us (1%)
    unnamed x5, waiting for transfers between devices  429 us
    psum x1, waiting for transfers between devices, shards(): down_total = lax.psum(down_part, 'head')  263 us
    psum x1, waiting for transfers between devices, shards(): lax.psum(jnp.dot(gated, out_weight, preferred_element_type=jnp.float32),...  243 us
    psum x1, waiting for transfers between devices, shards(): numer_sum, total_sum = lax.psum((numerator, denominator), 'head')  133 us
    all_gather x1, blocking collectives, shards(): everyone = lax.all_gather(finished, 'req', axis=0, tiled=True)  101 us
    psum x1, blocking collectives, shards(): lax.psum((jnp.sum(final_rows * final_rows, axis=-1), jnp.sum(final_rows *...  84.3 us
    psum x1, blocking collectives, shards(): numer_sum, total_sum = lax.psum((numerator, denominator), 'head')  62 us
    all_gather x1, blocking collectives, shards(): whole_rows = lax.all_gather(hidden, 'head', axis=1, tiled=True)  51.2 us
  transfers between devices with their start and end apart: 4, of which 4 were waited for; matrix products, arithmetic and copies ran while one was open for 0% of the time, Pallas kernels for 0%

commit v1 on v0

--- a/solution.py
+++ b/solution.py
@@ -94,10 +94,15 @@
     is_key = (head_place * block_count + jnp.arange(block_count, dtype=jnp.int32)) % 2 == 0
     keyed = rotate(rms_scale(projected_rows, k_gain), position)
     fresh = jnp.where(is_key[None, :, None], keyed, projected_rows).astype(jnp.bfloat16)
+
+    def update_plane(work_x, array_dim):
+        e_now = jnp.stack([work_x for _ in range(lax.axis_size("head"))], 0)
+        front = lax.all_to_all(e_now, "head", 0, 0)
+        x_next = jnp.concatenate(front, array_dim)
+        return x_next
+
     all_queries, all_fresh = (
-        lax.all_gather(
-            query_rows.reshape(count_of_rows, own_heads * head_width), "head", axis=1, tiled=True
-        ),
+        update_plane(query_rows.reshape(count_of_rows, own_heads * head_width), 1),
         lax.all_gather(
             fresh.reshape(count_of_rows, block_count * head_width), "head", axis=1, tiled=True
         ),

time: 1500 us -> 1580 us (1.053)
  waiting for transfers between devices: 1070 us -> 1170 us
  blocking collectives: 392 us -> 361 us
    psum x1, waiting for transfers between devices: 133 us -> 235 us  [shards(): numer_sum, total_sum = lax.psum((numerator, denominator), 'head')]
    all_gather x1 -> x0, blocking collectives: 33.8 us -> none  [shards(): lax.all_gather(query_rows.reshape(count_of_rows, own_heads * head_width),...]
  transfers between devices with their start and end apart: 4 -> 5, of which waited for: 4 -> 4; matrix products, arithmetic and copies ran while one was open for 0% -> 0% of each run, Pallas kernels for 0% -> 0%
where the time goes in v1:
time: 1580 us
  waiting for transfers between devices  1170 us (74%)
  blocking collectives  361 us (23%)
    unnamed x5, waiting for transfers between devices  429 us
    psum x1, waiting for transfers between devices, shards(): down_total = lax.psum(down_part, 'head')  263 us
    psum x1, waiting for transfers between devices, shards(): lax.psum(jnp.dot(gated, out_weight, preferred_element_type=jnp.float32),...  243 us
    psum x1, waiting for transfers between devices, shards(): numer_sum, total_sum = lax.psum((numerator, denominator), 'head')  235 us
    all_gather x1, blocking collectives, shards(): everyone = lax.all_gather(finished, 'req', axis=0, tiled=True)  101 us
    psum x1, blocking collectives, shards(): lax.psum((jnp.sum(final_rows * final_rows, axis=-1), jnp.sum(final_rows *...  84.3 us
    psum x1, blocking collectives, shards(): numer_sum, total_sum = lax.psum((numerator, denominator), 'head')  62 us
    all_gather x1, blocking collectives, shards(): whole_rows = lax.all_gather(hidden, 'head', axis=1, tiled=True)  51.2 us
  transfers between devices with their start and end apart: 5, of which 4 were waited for; matrix products, arithmetic and copies ran while one was open for 0% of the time, Pallas kernels for 0%

profile of v1, /device:TPU:1, one launch (start us, length us, event | category | flops | bytes accessed | tf_op | source)
XLA Modules:
  0.0 1577.5 jit_solution(15030720127550050280)
XLA Ops:
  7.2 51.2 %all_gather.9 = bf16[8,2048]{1,0:T(8,128)(2,1)S(1)} all-gather(bf16[8,128]{1,0:T(8,128)(2,1)} %param.23), channel_id=1, replica_groups=mesh['req'=32,'head'=16] {'head'}, dimensions={1}, use_global_device_ids=true | all-gather | bytes 34816 | tf_op jit(solution)/shard_map/all_gather | solution.py:83
  58.5 0.8 select_reduce_fusion
  59.3 1.3 fusion.70
  60.6 0.6 iota_compare_fusion.2
  61.2 2.0 select_reduce_fusion.2
  63.2 0.8 select_reduce_fusion.1
  64.8 1.4 multiply_reduce_fusion.2
  66.2 0.7 multiply_bitcast_fusion.1
  67.8 3.5 all-to-all-start
  71.3 1.4 multiply_reduce_fusion.1
  72.8 0.7 multiply_bitcast_fusion
  73.7 46.2 %all_gather.10 = bf16[8,2048]{1,0:T(8,128)(2,1)S(1)} all-gather(bf16[8,128]{1,0:T(8,128)(2,1)S(1)} %fusion.57), channel_id=1, replica_groups=mesh['req'=32,'head'=16] {'head'}, dimensions={1}, use_global_device_ids=true | all-gather | bytes 34816 | tf_op jit(solution)/shard_map/all_gather | solution.py:106
  120.7 1.2 copy_bitcast_fusion
  122.2 2.5 while.16
  122.2 0.7 add_compare_fusion.2
  123.5 0.6 add_compare_fusion.2
  125.3 62.0 %psum.43 = f32[8,16]{0,1:T(8,128)S(1)} all-reduce(f32[8,16]{0,1:T(8,128)S(1)} %bitcast.132), channel_id=1, replica_groups=mesh['req'=32,'head'=16] {'head'}, use_global_device_ids=true, to_apply=%region_11.12 | all-reduce | flops 128 | bytes 1024 | tf_op jit(solution)/shard_map/psum | solution.py:171
  188.3 234.9 %all-reduce.9.cloned.1.call-done = f32[8,16,128]{2,0,1:T(8,128)} async-done(((f32[8,16,128]{2,0,1:T(8,128)}), f32[8,16,128]{2,0,1:T(8,128)}) %all-reduce.9.cloned.1.call-update) | async-done | bytes 65552 | tf_op jit(solution)/shard_map/psum | solution.py:171
  423.2 1.7 fusion.20
  425.0 242.6 %all-reduce.11.cloned.1.call-done = f32[8,2048]{1,0:T(8,128)} async-done(((f32[8,2048]{1,0:T(8,128)}), f32[8,2048]{1,0:T(8,128)}) %all-reduce.11.cloned.1.call-update) | async-done | bytes 65552 | tf_op jit(solution)/shard_map/psum | solution.py:201
  667.6 1.0 multiply_reduce_fusion
  668.9 16.2 %all_to_all.24 = bf16[32,2,256]{2,1,0:T(2,128)(2,1)S(1)} all-to-all(bf16[32,2,256]{2,1,0:T(2,128)(2,1)S(1)} %reshape.329), channel_id=1, replica_groups=mesh['req'=32,'head'=16] {'req'}, dimensions={0} | all-to-all | bytes 65536 | tf_op jit(solution)/shard_map/all_to_all | solution.py:206
  685.3 0.9 fusion.27
  686.3 1.0 fusion.29
  687.3 1.3 dynamic-slice
  689.2 428.8 %all-reduce.15.cloned.1.call-done = (f32[256,384]{1,0:T(8,128)}, f32[256,384]{1,0:T(8,128)}) async-done(((f32[256,384]{1,0:T(8,128)}, f32[256,384]{1,0:T(8,128)}), (f32[256,384]{1,0:T(8,128)}, f32[256,384]{1,0:T(8,128)})) %all-reduce.15.cloned.1.call-update) | async-done | bytes 786448
  1118.0 1.7 fusion.35
  1120.4 263.3 %all-reduce.13.cloned.1.call-done = f32[8,2048]{1,0:T(8,128)} async-done(((f32[8,2048]{1,0:T(8,128)}), f32[8,2048]{1,0:T(8,128)}) %all-reduce.13.cloned.1.call-update) | async-done | bytes 65552 | tf_op jit(solution)/shard_map/psum | solution.py:215
  1383.7 0.7 add_convert_fusion
  1384.4 101.1 %all_gather.11 = bf16[256,128]{1,0:T(8,128)(2,1)S(1)} all-gather(bf16[8,128]{1,0:T(8,128)(2,1)S(1)} %add_convert_fusion), channel_id=1, replica_groups=mesh['req'=32,'head'=16] {'req'}, dimensions={0}, use_global_device_ids=true | all-gather | bytes 67584 | tf_op jit(solution)/shard_map/all_gather | solution.py:219
  1485.5 0.7 fusion.48
  1486.2 84.3 %all-reduce.3 = (f32[8]{0:T(128)S(1)}, f32[8]{0:T(128)S(1)}) all-reduce(f32[8]{0:T(128)S(1)} %get-tuple-element.204, f32[8]{0:T(128)S(1)} %get-tuple-element.203), channel_id=1, replica_groups=mesh['req'=32,'head'=16] {'head'}, use_global_device_ids=true, to_apply=%region_21.22 | all-reduce | flops 16 | bytes 128 | tf_op jit(solution)/shard_map/psum | solution.py:223
  (85 shorter events, 6.8 us)
Async XLA Ops:
  7.2 1110.9 %copy-start = (bf16[384,2048]{1,0:T(8,128)(2,1)S(1)}, bf16[384,2048]{1,0:T(8,128)(2,1)}, u32[]{:S(2)}) copy-start(bf16[384,2048]{1,0:T(8,128)(2,1)} %param.38) | copy-start | bytes 4718596
  7.2 113.5 %copy-start.3 = (bf16[1,256,8,128]{3,2,1,0:T(8,128)(2,1)S(1)}, bf16[1,256,8,128]{3,2,1,0:T(8,128)(2,1)}, u32[]{:S(2)}) copy-start(bf16[1,256,8,128]{3,2,1,0:T(8,128)(2,1)} %param.31) | copy-start | bytes 1572868
  67.8 54.3 %all-to-all-start = ((bf16[16,8,128]{2,1,0:T(8,128)(2,1)}), bf16[16,8,128]{2,1,0:T(8,128)(2,1)S(1)}, u32[]{:S(2)}, u32[]{:S(2)}) async-start(bf16[16,8,128]{2,1,0:T(8,128)(2,1)} %stack.3), calls=%async_computation | async-start | bytes 65536 | tf_op jit(solution)/shard_map/all_to_all | solution.py:100
  71.2 352.0 %all-reduce.9.cloned.1.call-start = ((), (), s32[]{:S(2)}) async-start(), calls=%async_computation.2 | async-start | bytes 131072 | tf_op jit(solution)/shard_map/psum | solution.py:171
  122.1 2.7 copy-start.10
  122.1 65.2 %copy-start.11 = (bf16[1,4,16,8,128]{4,3,2,1,0:T(8,128)(2,1)S(1)}, bf16[1,4,16,8,128]{4,3,2,1,0:T(8,128)(2,1)}, u32[]{:S(2)}) copy-start(bf16[1,4,16,8,128]{4,3,2,1,0:T(8,128)(2,1)} %param.34) | copy-start | bytes 393220
  122.1 301.0 %copy-start.4 = (f32[2048]{0:T(1024)S(1)}, f32[2048]{0:T(1024)}, u32[]{:S(2)}) copy-start(f32[2048]{0:T(1024)} %param.24) | copy-start | bytes 24580
  124.7 298.5 %copy-start.1 = (bf16[128,2048]{1,0:T(8,128)(2,1)S(1)}, bf16[128,2048]{1,0:T(8,128)(2,1)}, u32[]{:S(2)}) copy-start(bf16[128,2048]{1,0:T(8,128)(2,1)} %param.30) | copy-start | bytes 1572868
  124.7 298.5 %copy-start.2 = (bf16[2048,128]{1,0:T(8,128)(2,1)S(1)}, bf16[2048,128]{1,0:T(8,128)(2,1)}, u32[]{:S(2)}) copy-start(bf16[2048,128]{1,0:T(8,128)(2,1)} %param.26) | copy-start | bytes 1572868
  124.7 543.9 %copy-start.7 = (f32[2048]{0:T(1024)S(1)}, f32[2048]{0:T(1024)}, u32[]{:S(2)}) copy-start(f32[2048]{0:T(1024)} %param.35) | copy-start | bytes 24580
  125.1 560.2 %copy-start.5 = (bf16[64,384]{1,0:T(8,128)(2,1)S(1)}, bf16[64,384]{1,0:T(8,128)(2,1)}, u32[]{:S(2)}) copy-start(bf16[64,384]{1,0:T(8,128)(2,1)} %param.37) | copy-start | bytes 147460
  187.5 498.7 %copy-start.6 = (bf16[64,384]{1,0:T(8,128)(2,1)S(1)}, bf16[64,384]{1,0:T(8,128)(2,1)}, u32[]{:S(2)}) copy-start(bf16[64,384]{1,0:T(8,128)(2,1)} %param.36) | copy-start | bytes 147460
  188.2 479.4 %all-reduce.11.cloned.1.call-start = ((), (), s32[]{:S(2)}) async-start(), calls=%async_computation.3 | async-start | bytes 131072 | tf_op jit(solution)/shard_map/psum | solution.py:201
  424.9 693.1 %all-reduce.15.cloned.1.call-start = ((), (), s32[]{:S(2)}) async-start(), calls=%async_computation.5 | async-start | bytes 1572864
  686.2 799.2 %copy-start.8 = (f32[128]{0:T(128)S(1)}, f32[128]{0:T(128)}, u32[]{:S(2)}) copy-start(f32[128]{0:T(128)} %param.40) | copy-start | bytes 1540
  686.2 799.2 %copy-start.9 = (f32[128]{0:T(128)S(1)}, f32[128]{0:T(128)}, u32[]{:S(2)}) copy-start(f32[128]{0:T(128)} %param.39) | copy-start | bytes 1540
  687.2 696.4 %all-reduce.13.cloned.1.call-start = ((), (), s32[]{:S(2)}) async-start(), calls=%async_computation.4 | async-start | bytes 131072 | tf_op jit(solution)/shard_map/psum | solution.py:215
Sparse Core Ops, SparseCore 0:
  188.4 234.7 all-reduce.8
  426.3 241.2 all-reduce.10
  687.4 430.6 all-reduce.14
  1121.1 262.5 all-reduce.12
